TPU v7x, 32 devices: a whole 2x2x4 slice. The times are simulated.
32 devices in a mesh: dp: 8 (over y, x, core), tensor: 4 (over z).
Axes of the slice: x: 2, y: 2, z: 4, core: 2. Of those that a mesh axis runs over, the one named last changes fastest.
Arguments:
- activations: bfloat16 [2048, 8192], P('dp'), may hold values from -6 to 6
- out_grad: bfloat16 [2048, 2048], P('dp', 'tensor'), may hold values from -6 to 6
- weight: bfloat16 [8192, 2048], P(None, 'tensor'), may hold values from -0.0625 to 0.0625
- left_stats: float32 [8192, 2048], P('dp', 'tensor'), may hold values from -100 to 100, as said below
- right_stats: float32 [8192, 2048], P('dp', 'tensor'), may hold values from -100 to 100, as said below
Outputs:
- input_grad: bfloat16 [2048, 8192], P('dp', 'tensor')
- update: bfloat16 [8192, 2048], P('dp', 'tensor')
- left_new: float32 [8192, 2048], P('dp', 'tensor')
- right_new: float32 [8192, 2048], P('dp', 'tensor')
Inputs may be any that keep to these rules, and one draw needn't show every extreme that they name: `left_stats`: every 512 x 512 block at rows i * 512 and columns j * 512 is symmetric and positive definite. `right_stats`: every 512 x 512 block at rows i * 512 and columns j * 512 is symmetric and positive definite.
All inputs are finite; a program needn't handle non-finite values.
Results may differ from a plain program's by a relative error of at most 0.001.
Values may be sent and summed in bfloat16 or wider, within the bound.
A program may use at most 128 MiB of HBM per device.

v0:
```python
import jax
import jax.numpy as jnp
from jax import lax
from jax.sharding import PartitionSpec as P

BLOCK = 512
ITERS = 10


decay_rate = 0.9


def from_partner(value, axis, apart):
    mask = 2**apart
    pairs = [(source, source ^ mask) for source in range(lax.axis_size(axis))]
    return lax.ppermute(value, axis, pairs)


def batch_product(form, first, second):
    return jnp.einsum(form, first, second, precision=lax.Precision.HIGHEST)


def inverse_root(matrix):
    identity = jnp.eye(matrix.shape[-1], dtype=matrix.dtype)
    frobenius = jnp.sqrt(jnp.sum(matrix * matrix, axis=(1, 2), keepdims=True))
    current = matrix / frobenius
    result = jnp.broadcast_to(identity, matrix.shape)
    for iteration in range(ITERS):
        factor = (5.0 * identity - current) / 4.0
        result = batch_product("bij,bjk->bik", result, factor)
        squared = batch_product("bij,bjk->bik", factor, factor)
        fourth = batch_product("bij,bjk->bik", squared, squared)
        current = batch_product("bij,bjk->bik", fourth, current)
    return result / jnp.sqrt(jnp.sqrt(frobenius))


def both_roots(left_gram, right_gram):
    block_total = left_gram.shape[0]
    roots = inverse_root(jnp.concatenate([left_gram, right_gram], 0))
    return (roots[:block_total], roots[block_total:])


def split_blocks(whole_rows):
    row_total, col_total = whole_rows.shape
    shaped = whole_rows.reshape(row_total // BLOCK, BLOCK, col_total // BLOCK, BLOCK)
    return shaped.transpose(0, 2, 1, 3).reshape(-1, BLOCK, BLOCK)


def join_blocks(blocks, row_total, col_total):
    shaped = blocks.reshape(row_total // BLOCK, col_total // BLOCK, BLOCK, BLOCK)
    return shaped.transpose(0, 2, 1, 3).reshape(row_total, col_total)


def shards(activations, out_grad, weight, left_stats, right_stats):
    rows_local, cols_local = left_stats.shape
    dp_index = lax.axis_index("dp")
    tokens = activations.shape[0] * lax.axis_size("dp")
    spread = lax.all_to_all(activations, "dp", split_axis=1, concat_axis=0, tiled=True)
    summed = lax.dot_general(
        spread,
        lax.all_gather(out_grad, "dp", axis=0, tiled=True),
        (((0,), (0,)), ((), ())),
        preferred_element_type=jnp.float32,
    )
    grad_rows = summed * tokens ** (-0.5)
    partial_terms = lax.dot_general(
        out_grad, weight, (((1,), (1,)), ((), ())), preferred_element_type=jnp.float32
    )
    input_grad = lax.psum_scatter(partial_terms, "tensor", scatter_dimension=1, tiled=True).astype(
        jnp.bfloat16
    )
    paired = rows_local < BLOCK
    if paired:
        lower_half = dp_index % 2 == 0
        partner_pieces = from_partner((grad_rows, left_stats, right_stats), "dp", 0)

        def attach(own_part, peer_part):
            return jnp.where(
                lower_half,
                jnp.concatenate([own_part, peer_part], 0),
                jnp.concatenate([peer_part, own_part], 0),
            )

        grad_full = attach(grad_rows, partner_pieces[0])
        left_full = attach(left_stats, partner_pieces[1])
        right_full = attach(right_stats, partner_pieces[2])
    else:
        grad_full, left_full, right_full = (grad_rows, left_stats, right_stats)
    grad_blocks = split_blocks(grad_full)
    left_gram = (
        decay_rate * split_blocks(left_full)
        + batch_product("bik,bjk->bij", grad_blocks, grad_blocks) / BLOCK
    )
    right_gram = (
        decay_rate * split_blocks(right_full)
        + batch_product("bki,bkj->bij", grad_blocks, grad_blocks) / BLOCK
    )
    if paired:
        own_stat = jnp.where(lower_half, left_gram, right_gram)
        own_root = inverse_root(own_stat)
        partner_root = from_partner(own_root, "dp", 0)
        left_root = jnp.where(lower_half, own_root, partner_root)
        right_root = jnp.where(lower_half, partner_root, own_root)
    else:
        left_root, right_root = both_roots(left_gram, right_gram)
    update = batch_product(
        "bij,bjk->bik", batch_product("bij,bjk->bik", left_root, grad_blocks), right_root
    )
    row_total = grad_full.shape[0]
    update_rows = join_blocks(update, row_total, cols_local)
    left_rows = join_blocks(left_gram, row_total, cols_local)
    right_rows = join_blocks(right_gram, row_total, cols_local)
    if paired:
        offset = dp_index % 2 * rows_local
        update_rows = lax.dynamic_slice_in_dim(update_rows, offset, rows_local, 0)
        left_rows = lax.dynamic_slice_in_dim(left_rows, offset, rows_local, 0)
        right_rows = lax.dynamic_slice_in_dim(right_rows, offset, rows_local, 0)
    return (input_grad, update_rows.astype(jnp.bfloat16), left_rows, right_rows)


def solution(mesh):
    placed = (
        P("dp", None),
        P("dp", "tensor"),
        P(None, "tensor"),
        P("dp", "tensor"),
        P("dp", "tensor"),
    )
    return jax.shard_map(
        shards,
        mesh=mesh,
        in_specs=placed,
        out_specs=(P("dp", "tensor"), P("dp", "tensor"), P("dp", "tensor"), P("dp", "tensor")),
        check_vma=False,
    )
```

profile of v0, /device:TPU:0, one launch (start us, length us, event | category | flops | bytes accessed | tf_op | source)
XLA Modules:
  0.0 416.3 jit_solution(11902891883327772941)
XLA Ops:
  20.5 9.1 %fusion.94 = f32[256,8192]{1,0:T(8,128)} fusion(bf16[256,512]{1,0:T(8,128)(2,1)S(1)} %copy-done.8, bf16[8192,512]{1,0:T(8,128)(2,1)} %param.7), kind=kOutput, calls=%fused_computation.106 | convolution fusion | flops 2147483648 | bytes 17039360 | tf_op jit(solution)/shard_map/dot_general | solution.py:66
  34.7 43.3 %all-to-all-done = bf16[256,8,1024]{0,2,1:T(8,128)(2,1)} async-done(((bf16[256,8,1024]{0,2,1:T(8,128)(2,1)}), bf16[256,8,1024]{0,2,1:T(8,128)(2,1)}, u32[]{:S(2)}, u32[]{:S(2)}) %all-to-all-start) | async-done | bytes 4194336 | tf_op jit(solution)/shard_map/all_to_all | solution.py:58
  97.9 8.6 %fusion.3 = f32[4,512,512]{2,1,0:T(8,128)S(1)} fusion(f32[512,512]{1,0:T(8,128)S(1)} %fusion.68, f32[2,512,512]{2,1,0:T(8,128)S(1)} %multiply_add_fusion, f32[2,512,512]{2,1,0:T(8,128)S(1)} %multiply_add_fusion.1, f32[4]{0:T(128)S(1)} %get-tuple-element.4), kind=kOutput, calls=%fused_computation.14 | convolution fusion | flops 6446645248 | bytes 9437200 | tf_op jit(solution)/shard_map/bij,bjk->bik/dot_general | solution.py:20
  121.6 7.9 %fusion.5 = f32[4,512,512]{2,1,0:T(8,128)S(1)} fusion(f32[4,512,512]{2,1,0:T(8,128)S(1)} %fusion.90, f32[512,512]{1,0:T(8,128)S(1)} %fusion.68), kind=kOutput, calls=%fused_computation.16 | convolution fusion | flops 6444548096 | bytes 9437184 | tf_op jit(solution)/shard_map/bij,bjk->bik/dot_general | solution.py:20
  136.6 7.8 %fusion.97 = f32[4,512,512]{2,1,0:T(8,128)S(1)} fusion(f32[4,512,512]{2,1,0:T(8,128)S(1)} %fusion.96, f32[4,512,512]{2,1,0:T(8,128)S(1)} %fusion.90), kind=kOutput, calls=%fused_computation.109 | convolution fusion | flops 6442450944 | bytes 12582912 | tf_op jit(solution)/shard_map/bij,bjk->bik/dot_general | solution.py:20
  166.6 7.9 %fusion.9 = f32[4,512,512]{2,1,0:T(8,128)S(1)} fusion(f32[4,512,512]{2,1,0:T(8,128)S(1)} %fusion.99, f32[512,512]{1,0:T(8,128)S(1)} %fusion.68), kind=kOutput, calls=%fused_computation.20 | convolution fusion | flops 6444548096 | bytes 9437184 | tf_op jit(solution)/shard_map/bij,bjk->bik/dot_general | solution.py:20
  181.7 7.7 %fusion.101 = f32[4,512,512]{2,1,0:T(8,128)S(1)} fusion(f32[4,512,512]{2,1,0:T(8,128)S(1)} %fusion.100, f32[4,512,512]{2,1,0:T(8,128)S(1)} %fusion.99), kind=kOutput, calls=%fused_computation.113 | convolution fusion | flops 6442450944 | bytes 12582912 | tf_op jit(solution)/shard_map/bij,bjk->bik/dot_general | solution.py:20
  189.4 7.7 %fusion.11 = f32[4,512,512]{2,1,0:T(8,128)S(1)} fusion(f32[4,512,512]{2,1,0:T(8,128)S(1)} %fusion.101, f32[512,512]{1,0:T(8,128)S(1)} %fusion.68), kind=kOutput, calls=%fused_computation.22 | convolution fusion | flops 6444548096 | bytes 9437184 | tf_op jit(solution)/shard_map/bij,bjk->bik/dot_general | solution.py:20
  211.9 7.7 %fusion.13 = f32[4,512,512]{2,1,0:T(8,128)S(1)} fusion(f32[4,512,512]{2,1,0:T(8,128)S(1)} %fusion.103, f32[512,512]{1,0:T(8,128)S(1)} %fusion.68), kind=kOutput, calls=%fused_computation.24 | convolution fusion | flops 6444548096 | bytes 9437184 | tf_op jit(solution)/shard_map/bij,bjk->bik/dot_general | solution.py:20
  234.5 7.9 %fusion.15 = f32[4,512,512]{2,1,0:T(8,128)S(1)} fusion(f32[4,512,512]{2,1,0:T(8,128)S(1)} %fusion.105, f32[512,512]{1,0:T(8,128)S(1)} %fusion.68), kind=kOutput, calls=%fused_computation.26 | convolution fusion | flops 6444548096 | bytes 9437184 | tf_op jit(solution)/shard_map/bij,bjk->bik/dot_general | solution.py:20
  257.0 7.7 %fusion.17 = f32[4,512,512]{2,1,0:T(8,128)S(1)} fusion(f32[4,512,512]{2,1,0:T(8,128)S(1)} %fusion.107, f32[512,512]{1,0:T(8,128)S(1)} %fusion.68), kind=kOutput, calls=%fused_computation.28 | convolution fusion | flops 6444548096 | bytes 9437184 | tf_op jit(solution)/shard_map/bij,bjk->bik/dot_general | solution.py:20
  279.7 8.9 %fusion.19 = f32[4,512,512]{2,1,0:T(8,128)} fusion(f32[4,512,512]{2,1,0:T(8,128)S(1)} %fusion.109, f32[512,512]{1,0:T(8,128)S(1)} %fusion.68), kind=kOutput, calls=%fused_computation.30 | convolution fusion | flops 6444548096 | bytes 9437184 | tf_op jit(solution)/shard_map/bij,bjk->bik/dot_general | solution.py:20
  288.6 10.4 %fusion.110 = f32[4,512,512]{2,1,0:T(8,128)S(1)} fusion(f32[4,512,512]{2,1,0:T(8,128)} %fusion.19), kind=kOutput, calls=%fused_computation.122 | convolution fusion | flops 6442450944 | bytes 8388608 | tf_op jit(solution)/shard_map/bij,bjk->bik/dot_general | solution.py:20
  299.0 8.4 %fusion.111 = f32[4,512,512]{2,1,0:T(8,128)} fusion(f32[4,512,512]{2,1,0:T(8,128)S(1)} %fusion.110, f32[4,512,512]{2,1,0:T(8,128)S(1)} %fusion.109), kind=kOutput, calls=%fused_computation.123 | convolution fusion | flops 6442450944 | bytes 12582912 | tf_op jit(solution)/shard_map/bij,bjk->bik/dot_general | solution.py:20
  307.5 10.8 %fusion.4 = f32[4,512,512]{2,1,0:T(8,128)} fusion(f32[512,512]{1,0:T(8,128)S(1)} %fusion.68, f32[512,512]{1,0:T(8,128)S(1)} %copy-done.9, f32[2,512,512]{2,1,0:T(8,128)} %copy-done.1, f32[2,512,512]{2,1,0:T(8,128)} %copy-done.2, f32[4]{0:T(128)S(1)} %get-tuple-element.4), kind=kOutput, calls=%fused_computation.15 | convolution fusion | flops 6446645248 | bytes 10485776 | tf_op jit(solution)/shard_map/bij,bjk->bik/dot_general | solution.py:20
  318.2 12.0 %fusion.6 = f32[4,512,512]{2,1,0:T(8,128)} fusion(f32[4,512,512]{2,1,0:T(8,128)} %fusion.4, f32[4,512,512]{2,1,0:T(8,128)} %copy-done, f32[512,512]{1,0:T(8,128)S(1)} %fusion.68), kind=kOutput, calls=%fused_computation.17 | convolution fusion | flops 6444548096 | bytes 13631488 | tf_op jit(solution)/shard_map/bij,bjk->bik/dot_general | solution.py:20
  330.2 10.3 %fusion.8 = f32[4,512,512]{2,1,0:T(8,128)} fusion(f32[4,512,512]{2,1,0:T(8,128)} %fusion.6, f32[4,512,512]{2,1,0:T(8,128)S(1)} %fusion.97, f32[512,512]{1,0:T(8,128)S(1)} %fusion.68), kind=kOutput, calls=%fused_computation.19 | convolution fusion | flops 6444548096 | bytes 13631488 | tf_op jit(solution)/shard_map/bij,bjk->bik/dot_general | solution.py:20
  340.5 9.5 %fusion.10 = f32[4,512,512]{2,1,0:T(8,128)S(1)} fusion(f32[4,512,512]{2,1,0:T(8,128)} %fusion.8, f32[4,512,512]{2,1,0:T(8,128)S(1)} %fusion.99, f32[512,512]{1,0:T(8,128)S(1)} %fusion.68), kind=kOutput, calls=%fused_computation.21 | convolution fusion | flops 6444548096 | bytes 13631488 | tf_op jit(solution)/shard_map/bij,bjk->bik/dot_general | solution.py:20
  350.0 7.8 %fusion.12 = f32[4,512,512]{2,1,0:T(8,128)S(1)} fusion(f32[4,512,512]{2,1,0:T(8,128)S(1)} %fusion.10, f32[4,512,512]{2,1,0:T(8,128)S(1)} %fusion.101, f32[512,512]{1,0:T(8,128)S(1)} %fusion.68), kind=kOutput, calls=%fused_computation.23 | convolution fusion | flops 6444548096 | bytes 13631488 | tf_op jit(solution)/shard_map/bij,bjk->bik/dot_general | solution.py:20
  357.8 8.0 %fusion.14 = f32[4,512,512]{2,1,0:T(8,128)S(1)} fusion(f32[4,512,512]{2,1,0:T(8,128)S(1)} %fusion.12, f32[4,512,512]{2,1,0:T(8,128)S(1)} %fusion.103, f32[512,512]{1,0:T(8,128)S(1)} %fusion.68), kind=kOutput, calls=%fused_computation.25 | convolution fusion | flops 6444548096 | bytes 13631488 | tf_op jit(solution)/shard_map/bij,bjk->bik/dot_general | solution.py:20
  365.8 7.8 %fusion.16 = f32[4,512,512]{2,1,0:T(8,128)S(1)} fusion(f32[4,512,512]{2,1,0:T(8,128)S(1)} %fusion.14, f32[4,512,512]{2,1,0:T(8,128)S(1)} %fusion.105, f32[512,512]{1,0:T(8,128)S(1)} %fusion.68), kind=kOutput, calls=%fused_computation.27 | convolution fusion | flops 6444548096 | bytes 13631488 | tf_op jit(solution)/shard_map/bij,bjk->bik/dot_general | solution.py:20
  373.6 8.0 %fusion.18 = f32[4,512,512]{2,1,0:T(8,128)S(1)} fusion(f32[4,512,512]{2,1,0:T(8,128)S(1)} %fusion.16, f32[4,512,512]{2,1,0:T(8,128)S(1)} %fusion.107, f32[512,512]{1,0:T(8,128)S(1)} %fusion.68), kind=kOutput, calls=%fused_computation.29 | convolution fusion | flops 6444548096 | bytes 13631488 | tf_op jit(solution)/shard_map/bij,bjk->bik/dot_general | solution.py:20
  381.6 7.8 %fusion.20 = f32[4,512,512]{2,1,0:T(8,128)S(1)} fusion(f32[4,512,512]{2,1,0:T(8,128)S(1)} %fusion.18, f32[4,512,512]{2,1,0:T(8,128)S(1)} %fusion.109, f32[512,512]{1,0:T(8,128)S(1)} %fusion.68), kind=kOutput, calls=%fused_computation.31 | convolution fusion | flops 6444548096 | bytes 13631488 | tf_op jit(solution)/shard_map/bij,bjk->bik/dot_general | solution.py:20
  389.4 8.0 %broadcast_divide_fusion = f32[4,512,512]{2,1,0:T(8,128)S(1)} fusion(f32[4]{0:T(128)S(1)} %get-tuple-element.5, f32[4,512,512]{2,1,0:T(8,128)S(1)} %fusion.20, f32[4,512,512]{2,1,0:T(8,128)S(1)} %copy-done.5, f32[512,512]{1,0:T(8,128)S(1)} %fusion.68), kind=kOutput, calls=%fused_computation.35 | convolution fusion | flops 6445596672 | bytes 13631504 | tf_op jit(solution)/shard_map/bij,bjk->bik/dot_general | solution.py:20
  (56 shorter events, 159.0 us)
Async XLA Ops:
  8.0 76.6 %all-gather.2.cloned.1.call-start = ((), (), s32[]{:S(2)}) async-start(), calls=%async_computation.3 | async-start | bytes 2359296 | tf_op jit(solution)/shard_map/all_gather | solution.py:61
  15.1 5.4 %copy-start.8 = (bf16[256,512]{1,0:T(8,128)(2,1)S(1)}, bf16[256,512]{1,0:T(8,128)(2,1)}, u32[]{:S(2)}) copy-start(bf16[256,512]{1,0:T(8,128)(2,1)} %param.6) | copy-start | bytes 786436
  15.1 62.8 %all-to-all-start = ((bf16[256,8,1024]{0,2,1:T(8,128)(2,1)}), bf16[256,8,1024]{0,2,1:T(8,128)(2,1)}, u32[]{:S(2)}, u32[]{:S(2)}) async-start(bf16[256,8,1024]{0,2,1:T(8,128)(2,1)} %bitcast.67), calls=%async_computation.1 | async-start | bytes 8388608 | tf_op jit(solution)/shard_map/all_to_all | solution.py:58
  20.4 385.3 %reduce-scatter.2.cloned.1.call-start = ((), (), s32[]{:S(2)}) async-start(), calls=%async_computation.2 | async-start | bytes 10485760 | tf_op jit(solution)/shard_map/reduce_scatter | solution.py:69
  29.6 2.0 copy-start.6
  29.6 3.5 copy-start.7
  84.6 5.4 %copy-start.4 = (f32[1024,512]{1,0:T(8,128)S(1)}, f32[1024,512]{1,0:T(8,128)}, u32[]{:S(2)}) copy-start(f32[1024,512]{1,0:T(8,128)} %broadcast_multiply_fusion) | copy-start | bytes 6291460
  90.0 3.7 copy-start.3
  93.6 20.2 %copy-start.1 = (f32[2,512,512]{2,1,0:T(8,128)}, f32[2,512,512]{2,1,0:T(8,128)S(1)}, u32[]{:S(2)}) copy-start(f32[2,512,512]{2,1,0:T(8,128)S(1)} %multiply_add_fusion) | copy-start | bytes 6291460
  97.3 16.5 %copy-start.2 = (f32[2,512,512]{2,1,0:T(8,128)}, f32[2,512,512]{2,1,0:T(8,128)S(1)}, u32[]{:S(2)}) copy-start(f32[2,512,512]{2,1,0:T(8,128)S(1)} %multiply_add_fusion.1) | copy-start | bytes 6291460
  121.5 15.0 %copy-start = (f32[4,512,512]{2,1,0:T(8,128)}, f32[4,512,512]{2,1,0:T(8,128)S(1)}, u32[]{:S(2)}) copy-start(f32[4,512,512]{2,1,0:T(8,128)S(1)} %fusion.90) | copy-start | bytes 12582916
  299.0 8.4 %copy-start.9 = (f32[512,512]{1,0:T(8,128)S(1)}, f32[512,512]{1,0:T(8,128)}, u32[]{:S(2)}) copy-start(f32[512,512]{1,0:T(8,128)} %fusion.69) | copy-start | bytes 3145732
  381.6 7.8 %copy-start.5 = (f32[4,512,512]{2,1,0:T(8,128)S(1)}, f32[4,512,512]{2,1,0:T(8,128)}, u32[]{:S(2)}) copy-start(f32[4,512,512]{2,1,0:T(8,128)} %fusion.111) | copy-start | bytes 12582916
Sparse Core Ops, SparseCore 0:
  10.7 52.0 all-gather.1
Sparse Core Ops, SparseCore 1:
  29.7 146.8 reduce-scatter.1
where the time goes:
time: 420 us; the launch traced here: 416 us
  matrix products  329 us (78%)
  waiting for transfers between devices  44 us (10%)
  between operations  16.3 us (4%)
  local copies, waits for them, and re-layouts  13.8 us (3%)
  other arithmetic  7.55 us (2%)
  starting transfers between devices  5.38 us (1%)
    dot_general x41, matrix products, batch_product(): return jnp.einsum(form, first, second, precision=lax.Precision.HIGHEST)  315 us
    all_to_all x1, waiting for transfers between devices, shards(): lax.all_to_all(activations, 'dp', split_axis=1, concat_axis=0, tiled=True)  43.3 us
    dot_general x1, matrix products, shards(): lax.dot_general(out_grad, weight, (((1,), (1,)), ((), ())), preferred_ele...  9.08 us
  transfers between devices with their start and end apart: 3, of which 1 were waited for; matrix products, arithmetic and copies ran while one was open for 83% of the time, Pallas kernels for 0%

commit v1 on v0

v1 whole, which is shorter than its diff:
```python
import functools
import jax
import jax.numpy as jnp
from jax import lax
from jax.experimental import pallas as pl
from jax.experimental.pallas import tpu as pltpu
from jax.sharding import PartitionSpec as P

BLOCK = 512
ITERS = 10


decay_rate = 0.9


def from_partner(value, axis, apart):
    mask = 2**apart
    pairs = [(source, source ^ mask) for source in range(lax.axis_size(axis))]
    return lax.ppermute(value, axis, pairs)


def batch_product(form, first, second):
    return jnp.einsum(form, first, second, precision=lax.Precision.HIGH)


def parts(value):
    high = value.astype(jnp.bfloat16)
    return high, (value - high.astype(jnp.float32)).astype(jnp.bfloat16)


def product(first, second):
    (first_high, first_low), (second_high, second_low) = first, second
    return jnp.dot(
        jnp.concatenate([first_high, first_high, first_low], 1),
        jnp.concatenate([second_high, second_low, second_high], 0),
        preferred_element_type=jnp.float32,
    )


def root_kernel(count, *refs):
    ins, outs = refs[:count], refs[count : 2 * count]
    current_ref, result_ref = refs[2 * count :]
    order = ins[0].shape[-1]
    row = lax.broadcasted_iota(jnp.int32, (order, order), 0)
    col = lax.broadcasted_iota(jnp.int32, (order, order), 1)
    identity = (row == col).astype(jnp.float32)
    norms = []
    for place in range(count):
        matrix = ins[place][0]
        column_sums = jnp.sum(matrix * matrix, axis=0, keepdims=True)
        norms.append(jnp.sqrt(jnp.sum(column_sums, axis=1, keepdims=True)))
        current = matrix / norms[place]
        current_ref[place] = current
        result_ref[place] = (5.0 * identity - current) * 0.25

    def step(_, carry):
        for place in range(count):
            current = current_ref[place]
            first = parts(current)
            square = product(first, first)
            square_parts = parts(square)
            cube = product(square_parts, first)
            tail = product(square_parts, parts(cube - 20.0 * square))
            current = (625.0 * current - 500.0 * square + 150.0 * cube + tail) * (1.0 / 256.0)
            current_ref[place] = current
            result = result_ref[place]
            result_ref[place] = result + product(parts(result), parts((identity - current) * 0.25))
        return carry

    lax.fori_loop(0, ITERS - 1, step, 0)
    for place in range(count):
        outs[place][0] = result_ref[place] / jnp.sqrt(jnp.sqrt(norms[place]))


def inverse_roots(*matrices):
    count = len(matrices)
    total, order, _ = matrices[0].shape
    spec = pl.BlockSpec((1, order, order), lambda i: (i, 0, 0))
    return pl.pallas_call(
        functools.partial(root_kernel, count),
        grid=(total,),
        in_specs=[spec] * count,
        out_specs=[spec] * count,
        out_shape=[jax.ShapeDtypeStruct(m.shape, jnp.float32) for m in matrices],
        scratch_shapes=[pltpu.VMEM((count, order, order), jnp.float32)] * 2,
        compiler_params=pltpu.CompilerParams(vmem_limit_bytes=40 * 2**20),
        cost_estimate=pl.CostEstimate(
            flops=24 * count * total * (ITERS - 1) * order**3,
            bytes_accessed=8 * count * total * order**2,
            transcendentals=0,
        ),
    )(*matrices)


def split_blocks(whole_rows):
    row_total, col_total = whole_rows.shape
    shaped = whole_rows.reshape(row_total // BLOCK, BLOCK, col_total // BLOCK, BLOCK)
    return shaped.transpose(0, 2, 1, 3).reshape(-1, BLOCK, BLOCK)


def join_blocks(blocks, row_total, col_total):
    shaped = blocks.reshape(row_total // BLOCK, col_total // BLOCK, BLOCK, BLOCK)
    return shaped.transpose(0, 2, 1, 3).reshape(row_total, col_total)


def precondition(grad_rows, left_stats, right_stats):
    rows_local, cols_local = left_stats.shape
    dp_index = lax.axis_index("dp")
    paired = rows_local < BLOCK
    if paired:
        lower_half = dp_index % 2 == 0
        partner_pieces = from_partner((grad_rows, left_stats, right_stats), "dp", 0)

        def attach(own_part, peer_part):
            return jnp.where(
                lower_half,
                jnp.concatenate([own_part, peer_part], 0),
                jnp.concatenate([peer_part, own_part], 0),
            )

        grad_full = attach(grad_rows, partner_pieces[0])
        left_full = attach(left_stats, partner_pieces[1])
        right_full = attach(right_stats, partner_pieces[2])
    else:
        grad_full, left_full, right_full = (grad_rows, left_stats, right_stats)
    grad_blocks = split_blocks(grad_full)
    left_gram = (
        decay_rate * split_blocks(left_full)
        + batch_product("bik,bjk->bij", grad_blocks, grad_blocks) / BLOCK
    )
    right_gram = (
        decay_rate * split_blocks(right_full)
        + batch_product("bki,bkj->bij", grad_blocks, grad_blocks) / BLOCK
    )
    if paired:
        own_stat = jnp.where(lower_half, left_gram, right_gram)
        (own_root,) = inverse_roots(own_stat)
        partner_root = from_partner(own_root, "dp", 0)
        left_root = jnp.where(lower_half, own_root, partner_root)
        right_root = jnp.where(lower_half, partner_root, own_root)
    else:
        left_root, right_root = inverse_roots(left_gram, right_gram)
    update = batch_product(
        "bij,bjk->bik", batch_product("bij,bjk->bik", left_root, grad_blocks), right_root
    )
    row_total = grad_full.shape[0]
    update_rows = join_blocks(update, row_total, cols_local)
    left_rows = join_blocks(left_gram, row_total, cols_local)
    right_rows = join_blocks(right_gram, row_total, cols_local)
    if paired:
        offset = dp_index % 2 * rows_local
        update_rows = lax.dynamic_slice_in_dim(update_rows, offset, rows_local, 0)
        left_rows = lax.dynamic_slice_in_dim(left_rows, offset, rows_local, 0)
        right_rows = lax.dynamic_slice_in_dim(right_rows, offset, rows_local, 0)
    return (update_rows.astype(jnp.bfloat16), left_rows, right_rows)


def shards(activations, out_grad, weight, left_stats, right_stats):
    rows_local, cols_local = left_stats.shape
    dp_total = lax.axis_size("dp")
    tokens_local = activations.shape[0]
    scale = (tokens_local * dp_total) ** (-0.5)
    chunk_rows = min(rows_local, BLOCK)
    chunks = rows_local // chunk_rows
    pieces = activations.reshape(tokens_local, dp_total, chunks, chunk_rows)
    grads = lax.all_gather(out_grad, "dp", axis=0, tiled=True)
    spreads = [
        lax.all_to_all(
            pieces[:, :, chunk].reshape(tokens_local, dp_total * chunk_rows),
            "dp",
            split_axis=1,
            concat_axis=0,
            tiled=True,
        )
        for chunk in range(chunks)
    ]
    partial_terms = lax.dot_general(
        out_grad, weight, (((1,), (1,)), ((), ())), preferred_element_type=jnp.float32
    )
    input_grad = lax.psum_scatter(partial_terms, "tensor", scatter_dimension=1, tiled=True).astype(
        jnp.bfloat16
    )
    outs = []
    for chunk in range(chunks):
        summed = lax.dot_general(
            spreads[chunk], grads, (((0,), (0,)), ((), ())), preferred_element_type=jnp.float32
        )
        rows = slice(chunk * chunk_rows, (chunk + 1) * chunk_rows)
        outs.append(precondition(summed * scale, left_stats[rows], right_stats[rows]))
    joined = [jnp.concatenate(group, 0) for group in zip(*outs)]
    return (input_grad, *joined)


def solution(mesh):
    placed = (
        P("dp", None),
        P("dp", "tensor"),
        P(None, "tensor"),
        P("dp", "tensor"),
        P("dp", "tensor"),
    )
    return jax.shard_map(
        shards,
        mesh=mesh,
        in_specs=placed,
        out_specs=(P("dp", "tensor"), P("dp", "tensor"), P("dp", "tensor"), P("dp", "tensor")),
        check_vma=False,
    )
```

time: 420 us -> 235 us (0.56)
  matrix products: 329 us -> 24.6 us
  Pallas kernels: 0 us -> 135 us
  waiting for transfers between devices: 44 us -> 25.1 us
  starting transfers between devices: 5.38 us -> 10.6 us
    dot_general x42 -> x10, matrix products: 320 us -> 15.5 us  [the longest x8 8.21 us: batch_product(): return jnp.einsum(form, first, second, precision=lax.Precision.HIGH)]
    pallas_call x0 -> x2, Pallas kernels: none -> 135 us  [inverse_roots(): pl.pallas_call(functools.partial(root_kernel, count), grid=(total,), in_s...]
    all_to_all x1 -> x2, waiting for transfers between devices: 43.3 us -> 24.4 us  [shards(): lax.all_to_all(pieces[:, :, chunk].reshape(tokens_local, dp_total * chunk...]
    all_to_all x1 -> x2, starting transfers between devices: 5.3 us -> 10.5 us  [shards(): lax.all_to_all(pieces[:, :, chunk].reshape(tokens_local, dp_total * chunk...]
    all_to_all x1 -> x3, local copies, waits for them, and re-layouts: 6.63 us -> 10.2 us  [shards(): lax.all_to_all(pieces[:, :, chunk].reshape(tokens_local, dp_total * chunk...]
  transfers between devices with their start and end apart: 3 -> 4, of which waited for: 1 -> 1; matrix products, arithmetic and copies ran while one was open for 83% -> 19% of each run, Pallas kernels for 0% -> 57%
where the time goes in v1:
time: 235 us; the launch traced here: 234 us
  Pallas kernels  135 us (57%)
  waiting for transfers between devices  25.1 us (11%)
  matrix products  24.6 us (10%)
  local copies, waits for them, and re-layouts  17.7 us (8%)
  between operations  15.6 us (7%)
  starting transfers between devices  10.6 us (5%)
  other arithmetic  6.2 us (3%)
    pallas_call x2, Pallas kernels, inverse_roots(): pl.pallas_call(functools.partial(root_kernel, count), grid=(total,), in_s...  135 us
    all_to_all x2, waiting for transfers between devices, shards(): lax.all_to_all(pieces[:, :, chunk].reshape(tokens_local, dp_total * chunk...  24.4 us
    all_to_all x2, starting transfers between devices, shards(): lax.all_to_all(pieces[:, :, chunk].reshape(tokens_local, dp_total * chunk...  10.5 us
    all_to_all x3, local copies, waits for them, and re-layouts, shards(): lax.all_to_all(pieces[:, :, chunk].reshape(tokens_local, dp_total * chunk...  10.2 us
    dot_general x1, matrix products, shards(): lax.dot_general(out_grad, weight, (((1,), (1,)), ((), ())), preferred_ele...  9.08 us
    dot_general x8, matrix products, batch_product(): return jnp.einsum(form, first, second, precision=lax.Precision.HIGH)  8.21 us
    unnamed x9, local copies, waits for them, and re-layouts  7.49 us
    dot_general x2, matrix products, shards(): lax.dot_general(spreads[chunk], grads, (((0,), (0,)), ((), ())), preferre...  7.29 us
  transfers between devices with their start and end apart: 4, of which 1 were waited for; matrix products, arithmetic and copies ran while one was open for 19% of the time, Pallas kernels for 57%

profile of v1, /device:TPU:0, one launch (start us, length us, event | category | flops | bytes accessed | tf_op | source)
XLA Modules:
  0.0 234.4 jit_solution(7097391629885422077)
XLA Ops:
  8.0 0.7 all-gather.2.cloned.1.call-update
  8.8 9.1 %fusion.10 = f32[256,8192]{1,0:T(8,128)} fusion(bf16[256,512]{1,0:T(8,128)(2,1)} %param.6, bf16[8192,512]{1,0:T(8,128)(2,1)} %param.7), kind=kOutput, calls=%fused_computation.23 | convolution fusion | flops 2147483648 | bytes 17039360 | tf_op jit(solution)/shard_map/dot_general | solution.py:177
  17.9 6.4 %copy.16 = bf16[256,8192]{0,1:T(8,128)(2,1)} copy(bf16[256,8192]{1,0:T(8,128)(2,1)} %param.5) | data formatting | bytes 8388608 | tf_op args[0]
  24.3 3.9 %slice_bitcast_fusion.1 = (bf16[256,8,512]{0,2,1:T(8,128)(2,1)S(1)}, bf16[256,8,512]{0,2,1:T(8,128)(2,1)}) fusion(bf16[256,8,2,512]{0,3,2,1:T(8,128)(2,1)} %bitcast.49), kind=kLoop, calls=%fused_computation.1 | loop fusion | bytes 8388608 | tf_op jit(solution)/shard_map/all_to_all | solution.py:168
  28.2 3.9 %copy.20 = bf16[256,8,512]{2,0,1:T(8,128)(2,1)} copy(bf16[256,8,512]{0,2,1:T(8,128)(2,1)} %get-tuple-element.13) | data formatting | bytes 4194304 | tf_op jit(solution)/shard_map/all_to_all | solution.py:168
  32.1 6.0 %all-to-all-start.1 = ((bf16[256,8,512]{2,0,1:T(8,128)(2,1)}), bf16[256,8,512]{2,0,1:T(8,128)(2,1)}, u32[]{:S(2)}, u32[]{:S(2)}) async-start(bf16[256,8,512]{2,0,1:T(8,128)(2,1)} %copy.20), calls=%async_computation.2 | async-start | bytes 4194304 | tf_op jit(solution)/shard_map/all_to_all | solution.py:168
  38.1 2.4 %copy.18 = bf16[256,8,512]{2,0,1:T(8,128)(2,1)} copy(bf16[256,8,512]{0,2,1:T(8,128)(2,1)S(1)} %get-tuple-element.12) | data formatting | bytes 4194304 | tf_op jit(solution)/shard_map/all_to_all | solution.py:168
  40.5 24.4 %all-to-all-done.1 = bf16[256,8,512]{2,0,1:T(8,128)(2,1)} async-done(((bf16[256,8,512]{2,0,1:T(8,128)(2,1)}), bf16[256,8,512]{2,0,1:T(8,128)(2,1)}, u32[]{:S(2)}, u32[]{:S(2)}) %all-to-all-start.1) | async-done | bytes 2097184 | tf_op jit(solution)/shard_map/all_to_all | solution.py:168
  64.8 4.5 %all-to-all-start = ((bf16[256,8,512]{2,0,1:T(8,128)(2,1)}), bf16[256,8,512]{2,0,1:T(8,128)(2,1)}, u32[]{:S(2)}, u32[]{:S(2)}) async-start(bf16[256,8,512]{2,0,1:T(8,128)(2,1)} %copy.18), calls=%async_computation.1 | async-start | bytes 4194304 | tf_op jit(solution)/shard_map/all_to_all | solution.py:168
  69.4 3.6 %convolution_multiply_fusion.2 = f32[512,512]{1,0:T(8,128)S(1)} fusion(bf16[2048,512]{1,0:T(8,128)(2,1)} %bitcast.10, bf16[2048,512]{1,0:T(8,128)(2,1)} %all-gather.2.cloned.1.call-done), kind=kOutput, calls=%fused_computation.8 | convolution fusion | flops 1074003968 | bytes 5242880 | tf_op jit(solution)/shard_map/dot_general | solution.py:185
  73.1 1.0 fusion.1
  74.7 1.0 fusion
  75.7 67.3 %shard_map.85 = (f32[1,512,512]{2,1,0:T(8,128)S(1)}, f32[1,512,512]{2,1,0:T(8,128)S(1)}) custom-call(f32[1,512,512]{2,1,0:T(8,128)S(1)} %bitcast.45, f32[1,512,512]{2,1,0:T(8,128)S(1)} %bitcast.46), custom_call_target="tpu_custom_call" | custom-call | flops 57982058496 | bytes 4194304 | tf_op jit(solution)/shard_map/pallas_call | solution.py:79
  143.1 1.0 fusion.5
  144.1 1.0 convolution_convert_fusion
  145.1 3.6 %convolution_multiply_fusion.5 = f32[512,512]{1,0:T(8,128)S(1)} fusion(bf16[2048,512]{1,0:T(8,128)(2,1)} %bitcast.3, bf16[2048,512]{1,0:T(8,128)(2,1)} %all-gather.2.cloned.1.call-done), kind=kOutput, calls=%fused_computation.13 | convolution fusion | flops 1074003968 | bytes 5242880 | tf_op jit(solution)/shard_map/dot_general | solution.py:185
  148.8 1.0 fusion.3
  150.4 1.0 fusion.2
  151.4 67.3 %shard_map.84 = (f32[1,512,512]{2,1,0:T(8,128)S(1)}, f32[1,512,512]{2,1,0:T(8,128)S(1)}) custom-call(f32[1,512,512]{2,1,0:T(8,128)S(1)} %bitcast.47, f32[1,512,512]{2,1,0:T(8,128)S(1)} %bitcast.48), custom_call_target="tpu_custom_call" | custom-call | flops 57982058496 | bytes 4194304 | tf_op jit(solution)/shard_map/pallas_call | solution.py:79
  218.7 1.0 fusion.8
  219.7 1.0 convolution_convert_fusion.1
  220.7 1.0 pad_maximum_fusion.2
  221.8 2.4 %pad_maximum_fusion = (f32[1024,512]{1,0:T(8,128)}, f32[1024,512]{1,0:T(8,128)}) fusion(f32[512,512]{1,0:T(8,128)S(1)} %fusion.1, f32[512,512]{1,0:T(8,128)S(1)} %fusion.3, f32[512,512]{1,0:T(8,128)S(1)} %fusion, f32[512,512]{1,0:T(8,128)S(1)} %fusion.2), kind=kLoop, calls=%fused_computation.2 | loop fusion | flops 1048576 | bytes 8388608 | tf_op jit(solution)/shard_map/concatenate | solution.py:190
  224.2 2.7 %convert_element_type.9 = bf16[256,2048]{1,0:T(8,128)(2,1)} convert(f32[256,2048]{1,0:T(8,128)} %reduce-scatter.2.cloned.1.call-done) | non-fusion elementwise | flops 524288 | bytes 3145728 | tf_op jit(solution)/shard_map/convert_element_type | solution.py:180
  (14 shorter events, 1.2 us)
Async XLA Ops:
  8.0 61.4 %all-gather.2.cloned.1.call-start = ((), (), s32[]{:S(2)}) async-start(), calls=%async_computation.4 | async-start | bytes 2359296 | tf_op jit(solution)/shard_map/all_gather | solution.py:166
  8.7 215.5 %reduce-scatter.2.cloned.1.call-start = ((), (), s32[]{:S(2)}) async-start(), calls=%async_computation.3 | async-start | bytes 10485760 | tf_op jit(solution)/shard_map/reduce_scatter | solution.py:180
  32.1 32.8 %all-to-all-start.1 = ((bf16[256,8,512]{2,0,1:T(8,128)(2,1)}), bf16[256,8,512]{2,0,1:T(8,128)(2,1)}, u32[]{:S(2)}, u32[]{:S(2)}) async-start(bf16[256,8,512]{2,0,1:T(8,128)(2,1)} %copy.20), calls=%async_computation.2 | async-start | bytes 4194304 | tf_op jit(solution)/shard_map/all_to_all | solution.py:168
  64.8 80.3 %all-to-all-start = ((bf16[256,8,512]{2,0,1:T(8,128)(2,1)}), bf16[256,8,512]{2,0,1:T(8,128)(2,1)}, u32[]{:S(2)}, u32[]{:S(2)}) async-start(bf16[256,8,512]{2,0,1:T(8,128)(2,1)} %copy.18), calls=%async_computation.1 | async-start | bytes 4194304 | tf_op jit(solution)/shard_map/all_to_all | solution.py:168
  69.4 3.7 %copy-start = (f32[1024,512]{1,0:T(8,128)S(1)}, f32[1024,512]{1,0:T(8,128)}, u32[]{:S(2)}) copy-start(f32[1024,512]{1,0:T(8,128)} %param.8) | copy-start | bytes 6291460
  73.1 1.6 copy-start.2
  145.1 3.7 %copy-start.1 = (f32[1024,512]{1,0:T(8,128)S(1)}, f32[1024,512]{1,0:T(8,128)}, u32[]{:S(2)}) copy-start(f32[1024,512]{1,0:T(8,128)} %param.8) | copy-start | bytes 6291460
  148.8 1.6 copy-start.3
Sparse Core Ops, SparseCore 0:
  10.7 30.5 all-gather.1
Sparse Core Ops, SparseCore 1:
  18.0 147.1 reduce-scatter.1
